TPU v7x, 32 devices: a whole 2x2x4 slice. The times are simulated.
32 devices in a mesh: expert: 4 (over y, x), tp: 8 (over z, core).
Axes of the slice: x: 2, y: 2, z: 4, core: 2. Of those that a mesh axis runs over, the one named last changes fastest.
Arguments:
- tokens_in: bfloat16 [512, 3072], P(('expert', 'tp')), may hold values from -6 to 6
- grad_out: bfloat16 [512, 3072], P(('expert', 'tp')), may hold values from -6 to 6
- expert_ids: int32 [512, 2], P(('expert', 'tp')), may hold values from 0 to 3, all different within a row; in each aligned block of 16 rows (0 to 15, 16 to 31, ...) at most 8 rows name the same one
- combine: float32 [512, 2], P(('expert', 'tp')), may hold values from 0.2 to 1
- w_gate: bfloat16 [4, 3072, 8192], P('expert', None, 'tp'), may hold values from -0.109375 to 0.109375
- w_up: bfloat16 [4, 3072, 8192], P('expert', None, 'tp'), may hold values from -0.109375 to 0.109375
- w_down: bfloat16 [4, 8192, 3072], P('expert', 'tp'), may hold values from -0.0625 to 0.0625
Outputs:
- grad_input: bfloat16 [512, 3072], P(('expert', 'tp'))
- grad_gate: bfloat16 [4, 3072, 8192], P('expert', None, 'tp')
- grad_up: bfloat16 [4, 3072, 8192], P('expert', None, 'tp')
- grad_down: bfloat16 [4, 8192, 3072], P('expert', 'tp')
Inputs may be any that keep to these rules, and one draw needn't show every extreme that they name: `expert_ids`: the two ids of a row differ. In each aligned block of 16 rows (the tokens of one device) no expert is named by more than 8 rows, and some block names some expert exactly 8 times.
All inputs are finite; a program needn't handle non-finite values.
Results may differ from a plain program's by a relative error of at most 0.0065.
Values may be sent and summed in bfloat16 or wider, within the bound.
A program may use at most 128 MiB of HBM per device.

v0:
```python
import jax
import jax.numpy as jnp
from jax import lax
from jax.sharding import PartitionSpec as P


def positions(block_ids, groups):
    flat_ids = block_ids.reshape(-1)
    matches = (flat_ids[:, None] == jnp.arange(groups, dtype=jnp.int32)[None, :]).astype(jnp.int32)
    earlier = jnp.cumsum(matches, axis=0) - matches
    return jnp.sum(earlier * matches, axis=1)


def contract_rows(left, right):
    return lax.dot_general(
        left, right, (((0,), (0,)), ((), ())), preferred_element_type=jnp.float32
    )


def contract_cols(left, right):
    return lax.dot_general(
        left, right, (((1,), (1,)), ((), ())), preferred_element_type=jnp.float32
    )


def per_device(tokens_in, grad_out, expert_ids, combine, w_gate, w_up, w_down):
    groups = lax.axis_size("expert")
    local_tokens, width = tokens_in.shape
    capacity = local_tokens // 2
    slots = positions(expert_ids, groups)
    target = expert_ids.reshape(-1) * capacity + slots
    slot_index = jnp.arange(groups * capacity, dtype=jnp.int32)
    matches = (target[None, :] == slot_index[:, None]).astype(jnp.float32)
    select = matches.reshape(groups * capacity, local_tokens, 2)
    picker = jnp.sum(select, axis=2)
    weighted = jnp.sum(select * combine[None, :, :], axis=2)
    highest = lax.Precision.HIGHEST
    send_in = jnp.dot(picker, tokens_in.astype(jnp.float32), precision=highest).astype(jnp.bfloat16)
    send_grad = jnp.dot(weighted, grad_out.astype(jnp.float32), precision=highest).astype(
        jnp.bfloat16
    )
    middle_in, middle_grad = (
        lax.all_to_all(send_in, "expert", split_axis=0, concat_axis=0, tiled=True),
        lax.all_to_all(send_grad, "expert", split_axis=0, concat_axis=0, tiled=True),
    )
    rows_in, rows_grad = (
        lax.all_gather(middle_in, "tp", axis=0, tiled=True),
        lax.all_gather(middle_grad, "tp", axis=0, tiled=True),
    )
    gate_w = w_gate[0]
    up_w = w_up[0]
    down_w = w_down[0]
    gate_pre = jnp.dot(rows_in, gate_w, preferred_element_type=jnp.float32)
    up_pre = jnp.dot(rows_in, up_w, preferred_element_type=jnp.float32)
    sigmoid_gate = jax.nn.sigmoid(gate_pre)
    activated = gate_pre * sigmoid_gate
    hidden = (activated * up_pre).astype(jnp.bfloat16)
    grad_down = contract_rows(hidden, rows_grad).astype(jnp.bfloat16)
    grad_hidden = contract_cols(rows_grad, down_w)
    grad_gate_pre = (
        grad_hidden * up_pre * sigmoid_gate * (1.0 + gate_pre * (1.0 - sigmoid_gate))
    ).astype(jnp.bfloat16)
    grad_up_pre = (grad_hidden * activated).astype(jnp.bfloat16)
    grad_gate = contract_rows(rows_in, grad_gate_pre).astype(jnp.bfloat16)
    grad_up = contract_rows(rows_in, grad_up_pre).astype(jnp.bfloat16)
    own_rows = lax.psum_scatter(
        contract_cols(grad_gate_pre, gate_w) + contract_cols(grad_up_pre, up_w),
        "tp",
        scatter_dimension=0,
        tiled=True,
    )
    returned = lax.all_to_all(
        own_rows.astype(jnp.bfloat16), "expert", split_axis=0, concat_axis=0, tiled=True
    )
    grad_input = contract_rows(picker, returned.astype(jnp.float32)).astype(jnp.bfloat16)
    return (grad_input, grad_gate[None], grad_up[None], grad_down[None])


def solution(mesh):
    return jax.shard_map(
        per_device,
        mesh=mesh,
        in_specs=(
            P(("expert", "tp"), None),
            P(("expert", "tp"), None),
            P(("expert", "tp"), None),
            P(("expert", "tp"), None),
            P("expert", None, "tp"),
            P("expert", None, "tp"),
            P("expert", "tp", None),
        ),
        out_specs=(
            P(("expert", "tp"), None),
            P("expert", None, "tp"),
            P("expert", None, "tp"),
            P("expert", "tp", None),
        ),
        check_vma=False,
    )
```

profile of v0, /device:TPU:0, one launch (start us, length us, event | category | flops | bytes accessed | tf_op | source)
XLA Modules:
  0.0 146.8 jit_solution(4914511474710134898)
XLA Ops:
  7.2 0.8 copy.23
  8.2 0.2 select_reduce_fusion.1
  8.5 0.1 copy.24
  8.6 0.7 multiply_add_fusion
  9.3 0.8 select_reduce_fusion
  10.0 0.4 fusion.14
  10.4 10.6 %all_to_all.36 = bf16[4,8,3072]{2,1,0:T(8,128)(2,1)} all-to-all(bf16[4,8,3072]{2,1,0:T(8,128)(2,1)S(1)} %fusion.14), channel_id=1, replica_groups=mesh['expert'=4,'tp'=8] {'expert'}, dimensions={0} | all-to-all | bytes 393216 | tf_op jit(solution)/shard_map/all_to_all | solution.py:43
  21.1 1.2 fusion.13
  22.3 8.6 %all_to_all.37 = bf16[4,8,3072]{2,1,0:T(8,128)(2,1)} all-to-all(bf16[4,8,3072]{2,1,0:T(8,128)(2,1)S(1)} %fusion.13), channel_id=1, replica_groups=mesh['expert'=4,'tp'=8] {'expert'}, dimensions={0} | all-to-all | bytes 393216 | tf_op jit(solution)/shard_map/all_to_all | solution.py:44
  31.0 14.8 %all-gather.5.cloned.1.call-done = bf16[256,3072]{1,0:T(8,128)(2,1)} async-done(((bf16[32,3072]{1,0:T(8,128)(2,1)}), bf16[256,3072]{1,0:T(8,128)(2,1)}) %all-gather.5.cloned.1.call-update) | async-done | bytes 1572880 | tf_op jit(solution)/shard_map/all_gather | solution.py:47
  45.8 6.1 %fusion.2 = f32[256,1024]{1,0:T(8,128)} fusion(bf16[256,3072]{1,0:T(8,128)(2,1)} %all-gather.5.cloned.1.call-done, bf16[1,3072,1024]{2,1,0:T(8,128)(2,1)} %param.11), kind=kOutput, calls=%fused_computation.2 | convolution fusion | flops 1610612736 | bytes 8912896 | tf_op jit(solution)/shard_map/dot_general | solution.py:53
  51.9 5.7 %fusion.6 = f32[256,1024]{1,0:T(8,128)} fusion(bf16[256,3072]{1,0:T(8,128)(2,1)S(1)} %copy-done.1, bf16[1,3072,1024]{2,1,0:T(8,128)(2,1)} %param.12), kind=kOutput, calls=%fused_computation.6 | convolution fusion | flops 1610612736 | bytes 8912896 | tf_op jit(solution)/shard_map/dot_general | solution.py:54
  57.6 14.4 %all-gather.3.cloned.1.call-done = bf16[256,3072]{1,0:T(8,128)(2,1)} async-done(((bf16[32,3072]{1,0:T(8,128)(2,1)}), bf16[256,3072]{1,0:T(8,128)(2,1)}) %all-gather.3.cloned.1.call-update) | async-done | bytes 1572880 | tf_op jit(solution)/shard_map/all_gather | solution.py:48
  72.1 5.9 %multiply_convert_fusion.1 = (bf16[256,1024]{1,0:T(8,128)(2,1)S(1)}, bf16[256,1024]{1,0:T(8,128)(2,1)S(1)}) fusion(f32[256,1024]{1,0:T(8,128)} %fusion.2, f32[256,1024]{1,0:T(8,128)} %fusion.6, bf16[256,3072]{1,0:T(8,128)(2,1)} %all-gather.3.cloned.1.call-done, bf16[1,1024,3072]{2,1,0:T(8,128)(2,1)} %param.13), kind=kOutput, calls=%fused_computation.20 | convolution fusion | flops 1614020608 | bytes 11010048 | tf_op jit(solution)/shard_map/dot_general | solution.py:21
  77.9 4.6 %fusion = f32[256,3072]{1,0:T(8,128)S(1)} fusion(bf16[256,1024]{1,0:T(8,128)(2,1)S(1)} %get-tuple-element.7, bf16[1,3072,1024]{2,1,0:T(8,128)(2,1)} %param.11), kind=kOutput, calls=%fused_computation | convolution fusion | flops 1610612736 | bytes 9961472 | tf_op jit(solution)/shard_map/dot_general | solution.py:21
  82.5 6.3 %fusion.10 = f32[256,3072]{1,0:T(8,128)} fusion(f32[256,3072]{1,0:T(8,128)S(1)} %fusion, bf16[256,1024]{1,0:T(8,128)(2,1)S(1)} %get-tuple-element.6, bf16[1,3072,1024]{2,1,0:T(8,128)(2,1)} %param.12), kind=kOutput, calls=%fused_computation.13 | convolution fusion | flops 1611399168 | bytes 13107200 | tf_op jit(solution)/shard_map/dot_general | solution.py:21
  88.9 4.5 %convert_bitcast_fusion.1 = bf16[1,3072,1024]{2,1,0:T(8,128)(2,1)} fusion(bf16[256,3072]{1,0:T(8,128)(2,1)S(1)} %copy-done.1, bf16[256,1024]{1,0:T(8,128)(2,1)S(1)} %get-tuple-element.6), kind=kOutput, calls=%fused_computation.11 | convolution fusion | flops 1613758464 | bytes 8388608 | tf_op jit(solution)/shard_map/dot_general | solution.py:15
  93.5 4.6 %convert_bitcast_fusion = bf16[1,1024,3072]{2,1,0:T(8,128)(2,1)} fusion(bf16[256,3072]{1,0:T(8,128)(2,1)S(1)} %copy-done.2, f32[256,1024]{1,0:T(8,128)S(1)} %copy-done.4, f32[256,1024]{1,0:T(8,128)S(1)} %copy-done.3), kind=kOutput, calls=%fused_computation.10 | convolution fusion | flops 1615331328 | bytes 9961472 | tf_op jit(solution)/shard_map/dot_general | solution.py:15
  98.1 30.9 %reduce-scatter.2.cloned.1.call-done = f32[32,3072]{1,0:T(8,128)} async-done(((f32[256,3072]{1,0:T(8,128)}), f32[32,3072]{1,0:T(8,128)}) %reduce-scatter.2.cloned.1.call-update) | async-done | bytes 393232 | tf_op jit(solution)/shard_map/reduce_scatter | solution.py:66
  129.0 1.7 %convert_bitcast_fusion.3 = bf16[4,8,3072]{2,1,0:T(8,128)(2,1)} fusion(f32[32,3072]{1,0:T(8,128)} %reduce-scatter.2.cloned.1.call-done), kind=kLoop, calls=%fused_computation.25 | loop fusion | flops 98304 | bytes 589824 | tf_op jit(solution)/shard_map/all_to_all | solution.py:72
  130.6 3.6 %all-to-all-start.2 = ((bf16[4,8,3072]{2,1,0:T(8,128)(2,1)}), bf16[4,8,3072]{2,1,0:T(8,128)(2,1)S(1)}, u32[]{:S(2)}, u32[]{:S(2)}) async-start(bf16[4,8,3072]{2,1,0:T(8,128)(2,1)} %convert_bitcast_fusion.3), calls=%async_computation.3 | async-start | bytes 393216 | tf_op jit(solution)/shard_map/all_to_all | solution.py:72
  134.3 4.5 %convert_bitcast_fusion.2 = bf16[1,3072,1024]{2,1,0:T(8,128)(2,1)} fusion(bf16[256,3072]{1,0:T(8,128)(2,1)S(1)} %copy-done.1, bf16[256,1024]{1,0:T(8,128)(2,1)S(1)} %get-tuple-element.7), kind=kOutput, calls=%fused_computation.12 | convolution fusion | flops 1613758464 | bytes 8388608 | tf_op jit(solution)/shard_map/dot_general | solution.py:15
  138.8 0.7 all-to-all-done.2
  139.5 0.8 convolution_convert_fusion.2
  (20 shorter events, 0.5 us)
Async XLA Ops:
  7.2 2.9 %copy-start = (bf16[16,3072]{1,0:T(8,128)(2,1)S(1)}, bf16[16,3072]{1,0:T(8,128)(2,1)}, u32[]{:S(2)}) copy-start(bf16[16,3072]{1,0:T(8,128)(2,1)} %param.7) | copy-start | bytes 294916
  7.2 38.6 %all-gather.5.cloned.1.call-start = ((), (), s32[]{:S(2)}) async-start(), calls=%async_computation.5 | async-start | bytes 1769472 | tf_op jit(solution)/shard_map/all_gather | solution.py:47
  21.0 51.0 %all-gather.3.cloned.1.call-start = ((), (), s32[]{:S(2)}) async-start(), calls=%async_computation.4 | async-start | bytes 1769472 | tf_op jit(solution)/shard_map/all_gather | solution.py:48
  31.0 98.0 %reduce-scatter.2.cloned.1.call-start = ((), (), s32[]{:S(2)}) async-start(), calls=%async_computation.6 | async-start | bytes 3538944 | tf_op jit(solution)/shard_map/reduce_scatter | solution.py:66
  45.8 6.1 %copy-start.1 = (bf16[256,3072]{1,0:T(8,128)(2,1)S(1)}, bf16[256,3072]{1,0:T(8,128)(2,1)}, u32[]{:S(2)}) copy-start(bf16[256,3072]{1,0:T(8,128)(2,1)} %all-gather.5.cloned.1.call-done) | copy-start | bytes 4718596
  88.9 4.6 %copy-start.2 = (bf16[256,3072]{1,0:T(8,128)(2,1)S(1)}, bf16[256,3072]{1,0:T(8,128)(2,1)}, u32[]{:S(2)}) copy-start(bf16[256,3072]{1,0:T(8,128)(2,1)} %all-gather.3.cloned.1.call-done) | copy-start | bytes 4718596
  88.9 4.6 %copy-start.3 = (f32[256,1024]{1,0:T(8,128)S(1)}, f32[256,1024]{1,0:T(8,128)}, u32[]{:S(2)}) copy-start(f32[256,1024]{1,0:T(8,128)} %fusion.2) | copy-start | bytes 3145732
  88.9 4.6 %copy-start.4 = (f32[256,1024]{1,0:T(8,128)S(1)}, f32[256,1024]{1,0:T(8,128)}, u32[]{:S(2)}) copy-start(f32[256,1024]{1,0:T(8,128)} %fusion.6) | copy-start | bytes 3145732
  130.6 8.8 %all-to-all-start.2 = ((bf16[4,8,3072]{2,1,0:T(8,128)(2,1)}), bf16[4,8,3072]{2,1,0:T(8,128)(2,1)S(1)}, u32[]{:S(2)}, u32[]{:S(2)}) async-start(bf16[4,8,3072]{2,1,0:T(8,128)(2,1)} %convert_bitcast_fusion.3), calls=%async_computation.3 | async-start | bytes 393216 | tf_op jit(solution)/shard_map/all_to_all | solution.py:72
Sparse Core Ops, SparseCore 0:
  21.2 24.5 all-gather.4
  47.4 24.5 all-gather.2
  89.0 39.8 reduce-scatter.1
where the time goes:
time: 147 us
  waiting for transfers between devices  60.7 us (41%)
  matrix products  44.8 us (30%)
  blocking collectives  19.2 us (13%)
  between operations  13.8 us (9%)
  starting transfers between devices  3.76 us (3%)
  other arithmetic  3.45 us (2%)
    reduce_scatter x1, waiting for transfers between devices, per_device(): lax.psum_scatter(contract_cols(grad_gate_pre, gate_w) + contract_cols(gra...  30.9 us
    dot_general x3, matrix products, contract_cols(): lax.dot_general(left, right, (((1,), (1,)), ((), ())), preferred_element_...  16.8 us
    all_gather x1, waiting for transfers between devices, per_device(): lax.all_gather(middle_in, 'tp', axis=0, tiled=True)  14.8 us
    dot_general x4, matrix products, contract_rows(): lax.dot_general(left, right, (((0,), (0,)), ((), ())), preferred_element_...  14.5 us
    all_gather x1, waiting for transfers between devices, per_device(): lax.all_gather(middle_grad, 'tp', axis=0, tiled=True)  14.4 us
    all_to_all x1, blocking collectives, per_device(): lax.all_to_all(send_in, 'expert', split_axis=0, concat_axis=0, tiled=True)  10.6 us
    all_to_all x1, blocking collectives, per_device(): lax.all_to_all(send_grad, 'expert', split_axis=0, concat_axis=0, tiled=True)  8.6 us
    dot_general x1, matrix products, per_device(): gate_pre = jnp.dot(rows_in, gate_w, preferred_element_type=jnp.float32)  6.13 us
  transfers between devices with their start and end apart: 4, of which 4 were waited for; matrix products, arithmetic and copies ran while one was open for 18% of the time, Pallas kernels for 0%

commit v1 on v0

v1 whole, which is shorter than its diff:
```python
import functools

import jax
import jax.numpy as jnp
from jax import lax
from jax.experimental import pallas as pl
from jax.experimental.pallas import tpu as pltpu
from jax.sharding import PartitionSpec as P

F32, BF16 = jnp.float32, jnp.bfloat16
PIECES = 3
VMEM_BYTES = 60 * 1024 * 1024


def dot(left, right, on_left, on_right):
    return lax.dot_general(
        left, right, (((on_left,), (on_right,)), ((), ())), preferred_element_type=F32
    )


def routing(meta, experts, rows, tokens):
    slots = tokens // 4
    extent = (rows, tokens)
    row = lax.broadcasted_iota(jnp.int32, extent, 0)
    lane = lax.broadcasted_iota(jnp.int32, extent, 1)
    unit = jnp.zeros(extent, jnp.int32)
    for i in range(1, 2 * experts):
        unit = unit + (row >= i * slots).astype(jnp.int32)
    slot = (row - unit * slots).astype(F32)
    core = unit & 1
    expert = (unit >> 1).astype(F32)
    same = (core == (lane >= tokens // 2).astype(jnp.int32)).astype(F32)
    first = (meta[0:1, :tokens] == expert).astype(F32) * same
    second = (meta[1:2, :tokens] == expert).astype(F32) * same
    named = first + second
    before = lax.broadcasted_iota(jnp.int32, (tokens, tokens), 0) < lax.broadcasted_iota(
        jnp.int32, (tokens, tokens), 1
    )
    earlier = dot(named.astype(BF16), before.astype(F32).astype(BF16), 1, 0)
    picks = named * (earlier == slot).astype(F32)
    weight = jnp.sum(
        picks * (first * meta[2:3, :tokens] + second * meta[3:4, :tokens]), axis=1, keepdims=True
    )
    return picks, weight


def exchange(E, C, tok, grad, meta, wg_h, wu_h, wd_h,
             rin_o, rgr_o, hid_o, ggp_o, gup_o, gi_o,
             wg, wu, wd, swap, gath, metab, sendb, X, picks, hid, ggp, gup,
             sibs, sibr, part, ret, tokp, zr, fin, got,
             wsem, osem, sw_s, sw_r, ga_s, ga_r, me_s, me_r, ex_s, ex_r, sx_s, sx_r,
             si_s, si_r, pa_s, pa_r, to_s, to_r, fi_s, fi_r):
    n_tok, D = tok.shape
    R = C * E * n_tok
    F = wg.shape[1]
    W = D // 2
    cw = W // PIECES
    e = lax.axis_index("expert")
    t = lax.axis_index("tp")
    z, c = t // 2, t % 2
    o = 1 - c

    def remote(src, dst, ssem, rsem, expert, tp):
        return pltpu.make_async_remote_copy(
            src_ref=src, dst_ref=dst, send_sem=ssem, recv_sem=rsem,
            device_id={"expert": expert, "tp": tp}, device_id_type=pl.DeviceIdType.MESH)

    sib = z * 2 + o
    weights = [pltpu.make_async_copy(a.at[0], b, wsem.at[i])
               for i, (a, b) in enumerate(((wg_h, wg), (wu_h, wu), (wd_h, wd)))]
    for w in weights:
        w.start()

    peers = [lax.rem(e + i, E) for i in range(1, E)]
    chips = [lax.rem(z + i, C) for i in range(1, C)]
    barrier = pltpu.get_barrier_semaphore()

    def hello(expert, tp):
        pl.semaphore_signal(barrier, inc=1, device_id={"expert": expert, "tp": tp},
                            device_id_type=pl.DeviceIdType.MESH)
    hello(e, sib)
    for q in peers:
        hello(q, t)
    for q in chips:
        hello(e, q * 2 + c)
    pl.semaphore_wait(barrier, 1 + (E - 1) + (C - 1))

    is_in = c == 0
    swap[...] = jnp.where(is_in, grad[...].astype(F32), tok[...].astype(F32)).astype(BF16)
    gath[z, c] = jnp.where(is_in, tok[...].astype(F32), grad[...].astype(F32)).astype(BF16)
    metab[z, c] = meta[...]
    a = remote(swap, gath.at[z, c], sw_s.at[0], sw_r.at[0], e, sib)
    b = remote(metab.at[z, c], metab.at[z, c], sw_s.at[1], sw_r.at[1], e, sib)
    a.start()
    b.start()
    a.wait_recv()
    b.wait_recv()

    def hop(origin, way):
        tp = (z + (1 if way == 0 else -1)) * 2 + c
        return (remote(gath.at[origin], gath.at[origin], ga_s.at[origin, way], ga_r.at[origin], e, tp),
                remote(metab.at[origin], metab.at[origin], me_s.at[origin, way], me_r.at[origin], e, tp))

    def send_on(origin, way):
        for d in hop(origin, way):
            d.start()

    can = (z + 1 < C, z >= 1)
    for way in (0, 1):
        pl.when(can[way])(functools.partial(send_on, z, way))

    def rows_out(origin, i):
        return remote(sendb.at[origin, peers[i]], X.at[c, origin, e],
                      ex_s.at[origin, i], ex_r.at[origin, i], peers[i], t)

    def process(origin):
        info = metab[origin, 0] + metab[origin, 1]
        sel, weight = routing(info, E, E * n_tok, 2 * n_tok)
        sel = sel.astype(BF16)
        picks[origin] = sel
        scale = jnp.where(is_in, jnp.ones_like(weight), weight)
        rows = dot(sel, gath[origin].reshape(2 * n_tok, D), 1, 0)
        sendb[origin] = (rows * scale).astype(BF16).reshape(E, n_tok, D)
        for i in range(E - 1):
            rows_out(origin, i).start()
        X[c, origin, e] = sendb[origin, e]

    def sibling_rows(kind, origin):
        return remote(X.at[kind, origin], X.at[kind, origin], sx_s.at[origin], sx_r.at[origin], e, sib)

    def arrived(origin):
        for i in range(E - 1):
            rows_out(origin, i).wait_recv()
        sibling_rows(c, origin).start()

    def take(origin, way):
        for d in hop(origin, way):
            d.wait_recv()
        pl.when(can[way])(functools.partial(send_on, origin, way))
        process(origin)

    process(z)
    for k in range(1, C):
        pl.when(z - k >= 0)(functools.partial(take, z - k, 0))
        pl.when(z + k < C)(functools.partial(take, z + k, 1))
    arrived(z)
    for k in range(1, C):
        pl.when(z - k >= 0)(functools.partial(arrived, z - k))
        pl.when(z + k < C)(functools.partial(arrived, z + k))
    for q in range(C):
        sibling_rows(o, q).wait_recv()
    for w in weights:
        w.wait()

    saves = [pltpu.make_async_copy(X.at[0], rin_o, osem.at[0]),
             pltpu.make_async_copy(X.at[1], rgr_o, osem.at[1])]
    for s in saves:
        s.start()

    step = min(256, F)

    @pl.loop(0, F // step)
    def _(n):
        cols = pl.ds(pl.multiple_of(n * step, step), step)
        rin = X[0].reshape(R, D)
        rgr = X[1].reshape(R, D)
        gate = dot(rin, wg[:, cols], 1, 0)
        up = dot(rin, wu[:, cols], 1, 0)
        gh = dot(rgr, wd[cols, :], 1, 1)
        s = jax.nn.sigmoid(gate)
        act = gate * s
        hid[:, cols] = (act * up).astype(BF16)
        ggp[:, cols] = (gh * up * s * (1.0 + gate * (1.0 - s))).astype(BF16)
        gup[:, cols] = (gh * act).astype(BF16)

    more = [pltpu.make_async_copy(a, b, osem.at[2 + i])
            for i, (a, b) in enumerate(((hid, hid_o), (ggp, ggp_o), (gup, gup_o)))]
    for s in more:
        s.start()
    saves += more

    def back(half, n):
        at = pl.ds(pl.multiple_of(half * W + n * cw, cw), cw)
        return dot(ggp[...], wg[at, :], 1, 1) + dot(gup[...], wu[at, :], 1, 1)

    def sib_sum(n):
        return remote(sibs.at[n], sibr.at[n], si_s.at[n], si_r.at[n], e, sib)

    def part_out(n, i):
        return remote(part.at[n, :, peers[i]], ret.at[n, e], pa_s.at[n, i], pa_r.at[n, i], peers[i], t)

    def tok_out(n, i):
        return remote(tokp.at[n, chips[i]], zr.at[n, z], to_s.at[n, i], to_r.at[n, i], e, chips[i] * 2 + c)

    def fin_out(n):
        return remote(fin.at[n, o], got.at[n], fi_s.at[n], fi_r.at[n], e, sib)

    for n in range(PIECES):
        sibs[n] = back(o, n).astype(BF16)
        sib_sum(n).start()
    for n in range(PIECES):
        own = back(c, n)
        sib_sum(n).wait_recv()
        part[n] = (own + sibr[n].astype(F32)).astype(BF16).reshape(C, E, n_tok, cw)
        for i in range(E - 1):
            part_out(n, i).start()
        ret[n, e] = part[n, :, e]

    def to_tokens(n, q):
        return dot(picks[q], ret[n, :, q].reshape(E * n_tok, cw), 0, 0)

    for n in range(PIECES):
        for i in range(E - 1):
            part_out(n, i).wait_recv()
        for i in range(C - 1):
            tokp[n, chips[i]] = to_tokens(n, chips[i]).astype(BF16).reshape(2, n_tok, cw)
            tok_out(n, i).start()
    for n in range(PIECES):
        total = to_tokens(n, z)
        for i in range(C - 1):
            tok_out(n, i).wait_recv()
        for i in range(C - 1):
            total = total + zr[n, chips[i]].astype(F32).reshape(2 * n_tok, cw)
        fin[n] = total.astype(BF16).reshape(2, n_tok, cw)
        fin_out(n).start()
        gi_o[:, pl.ds(pl.multiple_of(c * W + n * cw, cw), cw)] = fin[n, c]
    for n in range(PIECES):
        fin_out(n).wait_recv()
        gi_o[:, pl.ds(pl.multiple_of(o * W + n * cw, cw), cw)] = got[n]

    a.wait_send()
    b.wait_send()

    def sent(origin, way):
        for d in hop(origin, way):
            d.wait_send()

    for way in (0, 1):
        pl.when(can[way])(functools.partial(sent, z, way))
    for k in range(1, C):
        pl.when(jnp.logical_and(z - k >= 0, can[0]))(functools.partial(sent, z - k, 0))
        pl.when(jnp.logical_and(z + k < C, can[1]))(functools.partial(sent, z + k, 1))
    for q in range(C):
        for i in range(E - 1):
            rows_out(q, i).wait_send()
        sibling_rows(c, q).wait_send()
    for n in range(PIECES):
        sib_sum(n).wait_send()
        for i in range(E - 1):
            part_out(n, i).wait_send()
        for i in range(C - 1):
            tok_out(n, i).wait_send()
        fin_out(n).wait_send()
    for s in saves:
        s.wait()


def weight_grads(rin, rgr, hid, ggp, gup, gg, gu, gd):
    x = rin[...]
    gg[0] = dot(x, ggp[...], 0, 0).astype(BF16)
    gu[0] = dot(x, gup[...], 0, 0).astype(BF16)
    gd[0] = dot(hid[...], rgr[...], 0, 0).astype(BF16)


def per_device(E, T, tokens_in, grad_out, expert_ids, combine, w_gate, w_up, w_down):
    n_tok, D = tokens_in.shape
    F = w_gate.shape[2]
    C = T // 2
    R = C * E * n_tok
    cw = D // 2 // PIECES
    small = jnp.concatenate([expert_ids.T.astype(F32), combine.T], axis=0)
    core = lax.axis_index("tp") % 2
    wide = jnp.concatenate([jnp.where(core == 0, small, 0.0), jnp.where(core == 1, small, 0.0)], axis=1)
    meta = jnp.pad(wide, ((0, 4), (0, 128 - 2 * n_tok)))
    any_, vm = pl.BlockSpec(memory_space=pl.ANY), pl.BlockSpec(memory_space=pltpu.VMEM)
    rows_t = jax.ShapeDtypeStruct((C, E, n_tok, D), BF16)
    ff_t = jax.ShapeDtypeStruct((R, F), BF16)
    V, S = pltpu.VMEM, pltpu.SemaphoreType.DMA
    rin, rgr, hid, ggp, gup, grad_input = pl.pallas_call(
        functools.partial(exchange, E, C),
        out_shape=(rows_t, rows_t, ff_t, ff_t, ff_t, jax.ShapeDtypeStruct((n_tok, D), BF16)),
        in_specs=[vm, vm, vm, any_, any_, any_],
        out_specs=(any_, any_, any_, any_, any_, vm),
        scratch_shapes=[
            V((D, F), BF16), V((D, F), BF16), V((F, D), BF16),
            V((n_tok, D), BF16), V((C, 2, n_tok, D), BF16), V((C, 2, 8, 128), F32),
            V((C, E, n_tok, D), BF16), V((2, C, E, n_tok, D), BF16),
            V((C, E * n_tok, 2 * n_tok), BF16),
            V((R, F), BF16), V((R, F), BF16), V((R, F), BF16),
            V((PIECES, R, cw), BF16), V((PIECES, R, cw), BF16),
            V((PIECES, C, E, n_tok, cw), BF16), V((PIECES, E, C, n_tok, cw), BF16),
            V((PIECES, C, 2, n_tok, cw), BF16), V((PIECES, C, 2, n_tok, cw), BF16),
            V((PIECES, 2, n_tok, cw), BF16), V((PIECES, n_tok, cw), BF16),
            S((3,)), S((5,)), S((2,)), S((2,)),
            S((C, 2)), S((C,)), S((C, 2)), S((C,)),
            S((C, E - 1)), S((C, E - 1)), S((C,)), S((C,)),
            S((PIECES,)), S((PIECES,)), S((PIECES, E - 1)), S((PIECES, E - 1)),
            S((PIECES, C - 1)), S((PIECES, C - 1)), S((PIECES,)), S((PIECES,)),
        ],
        compiler_params=pltpu.CompilerParams(
            collective_id=0, has_side_effects=True, vmem_limit_bytes=VMEM_BYTES),
        cost_estimate=pl.CostEstimate(
            flops=10 * R * D * F, bytes_accessed=6 * D * F, transcendentals=R * F),
        name="exchange",
    )(tokens_in, grad_out, meta, w_gate, w_up, w_down)
    block = 512
    whole = pl.BlockSpec((R, F), lambda i: (0, 0))
    cols = pl.BlockSpec((R, block), lambda i: (0, i))
    gg, gu, gd = pl.pallas_call(
        weight_grads,
        grid=(D // block,),
        out_shape=(jax.ShapeDtypeStruct((1, D, F), BF16), jax.ShapeDtypeStruct((1, D, F), BF16),
                   jax.ShapeDtypeStruct((1, F, D), BF16)),
        in_specs=[cols, cols, whole, whole, whole],
        out_specs=(pl.BlockSpec((1, block, F), lambda i: (0, i, 0)),
                   pl.BlockSpec((1, block, F), lambda i: (0, i, 0)),
                   pl.BlockSpec((1, F, block), lambda i: (0, 0, i))),
        compiler_params=pltpu.CompilerParams(vmem_limit_bytes=VMEM_BYTES // 2),
        cost_estimate=pl.CostEstimate(
            flops=6 * R * D * F, bytes_accessed=6 * D * F, transcendentals=0),
        name="weight_grads",
    )(rin.reshape(R, D), rgr.reshape(R, D), hid, ggp, gup)
    return grad_input, gg, gu, gd


def solution(mesh):
    rows = P(("expert", "tp"), None)
    columns = P("expert", None, "tp")
    return jax.shard_map(
        functools.partial(per_device, mesh.shape["expert"], mesh.shape["tp"]),
        mesh=mesh,
        in_specs=(rows, rows, rows, rows, columns, columns, P("expert", "tp", None)),
        out_specs=(rows, columns, columns, P("expert", "tp", None)),
        check_vma=False,
    )
```

time: 147 us -> 77.3 us (0.53)
  Pallas kernels: 0 us -> 67.6 us
  waiting for transfers between devices: 60.7 us -> 0 us
  matrix products: 44.8 us -> 0 us
  blocking collectives: 19.2 us -> 0 us
  between operations: 13.8 us -> 0.67 us
  local copies, waits for them, and re-layouts: 1.04 us -> 6.58 us
  starting transfers between devices: 3.76 us -> 0 us
    pallas_call x0 -> x2, Pallas kernels: none -> 67.6 us  [the longest x1 59.3 us: per_device(): pl.pallas_call(functools.partial(exchange, E, C), out_shape=(rows_t, rows...]
    dot_general x11 -> x0, matrix products: 44.8 us -> none  [the longest x3 16.8 us: contract_cols(): lax.dot_general(left, right, (((1,), (1,)), ((), ())), preferred_element_...]
    reduce_scatter x1 -> x0, waiting for transfers between devices: 30.9 us -> none  [per_device(): lax.psum_scatter(contract_cols(grad_gate_pre, gate_w) + contract_cols(gra...]
    all_gather x2 -> x0, waiting for transfers between devices: 29.2 us -> none  [the longest x1 14.8 us: per_device(): lax.all_gather(middle_in, 'tp', axis=0, tiled=True)]
    all_to_all x2 -> x0, blocking collectives: 19.2 us -> none  [the longest x1 10.6 us: per_device(): lax.all_to_all(send_in, 'expert', split_axis=0, concat_axis=0, tiled=True)]
    unnamed x11 -> x13, local copies, waits for them, and re-layouts: 0.79 us -> 6.58 us
    all_to_all x1 -> x0, starting transfers between devices: 3.63 us -> none  [per_device(): lax.all_to_all(own_rows.astype(jnp.bfloat16), 'expert', split_axis=0, con...]
    all_to_all x1 -> x0, other arithmetic: 1.69 us -> none  [per_device(): lax.all_to_all(own_rows.astype(jnp.bfloat16), 'expert', split_axis=0, con...]
  transfers between devices with their start and end apart: 4 -> 0, of which waited for: 4 -> 0; matrix products, arithmetic and copies ran while one was open for 18% -> 0% of each run, Pallas kernels for 0% -> 0%
where the time goes in v1:
time: 77.3 us; the launch traced here: 76.9 us
  Pallas kernels  67.6 us (87%)
  local copies, waits for them, and re-layouts  6.58 us (9%)
  other arithmetic  2.04 us (3%)
    pallas_call x1, Pallas kernels, per_device(): pl.pallas_call(functools.partial(exchange, E, C), out_shape=(rows_t, rows...  59.3 us
    pallas_call x1, Pallas kernels, per_device(): pl.pallas_call(weight_grads, grid=(D // block,), out_shape=(jax.ShapeDtyp...  8.26 us
    unnamed x13, local copies, waits for them, and re-layouts  6.58 us

profile of v1, /device:TPU:0, one launch (start us, length us, event | category | flops | bytes accessed | tf_op | source)
XLA Modules:
  0.0 76.9 jit_solution(6217981196647627912)
XLA Ops:
  0.6 0.7 convert_bitcast_fusion
  1.3 0.7 fusion.1
  2.0 0.7 select_maximum_fusion.meta
  2.7 59.3 %exchange.1 = (bf16[4,4,16,3072]{3,2,1,0:T(8,128)(2,1)}, bf16[4,4,16,3072]{3,2,1,0:T(8,128)(2,1)}, bf16[256,1024]{1,0:T(8,128)(2,1)}, bf16[256,1024]{1,0:T(8,128...) custom-call(bf16[16,3072]{1,0:T(8,128)(2,1)} %tok.1, bf16[16,3072]{1,0:T(8,128)(2,1)} %grad.1, ...), custom_call_target="tpu_custom_call" | custom-call | flops 8053063680 | bytes 18874368 | tf_op jit(solution)/shard_map/exchange/pallas_call | solution.py:279
  62.0 0.0 copy-start
  62.0 1.4 %copy-done = bf16[4,4,16,3072]{3,2,1,0:T(8,128)(2,1)S(1)} copy-done((bf16[4,4,16,3072]{3,2,1,0:T(8,128)(2,1)S(1)}, bf16[4,4,16,3072]{3,2,1,0:T(8,128)(2,1)}, u32[]{:S(2)}) %copy-start) | copy-done | bytes 1572888
  63.4 0.0 copy-start.1
  63.4 1.4 %copy-done.1 = bf16[4,4,16,3072]{3,2,1,0:T(8,128)(2,1)S(1)} copy-done((bf16[4,4,16,3072]{3,2,1,0:T(8,128)(2,1)S(1)}, bf16[4,4,16,3072]{3,2,1,0:T(8,128)(2,1)}, u32[]{:S(2)}) %copy-start.1) | copy-done | bytes 1572888
  64.9 0.0 copy-start.2
  64.9 1.0 %copy-done.2 = bf16[256,1024]{1,0:T(8,128)(2,1)S(1)} copy-done((bf16[256,1024]{1,0:T(8,128)(2,1)S(1)}, bf16[256,1024]{1,0:T(8,128)(2,1)}, u32[]{:S(2)}) %copy-start.2) | copy-done | bytes 524312
  65.9 0.0 copy-start.3
  65.9 1.0 %copy-done.3 = bf16[256,1024]{1,0:T(8,128)(2,1)S(1)} copy-done((bf16[256,1024]{1,0:T(8,128)(2,1)S(1)}, bf16[256,1024]{1,0:T(8,128)(2,1)}, u32[]{:S(2)}) %copy-start.3) | copy-done | bytes 524312
  66.9 0.0 copy-start.4
  66.9 1.0 %copy-done.4 = bf16[256,1024]{1,0:T(8,128)(2,1)S(1)} copy-done((bf16[256,1024]{1,0:T(8,128)(2,1)S(1)}, bf16[256,1024]{1,0:T(8,128)(2,1)}, u32[]{:S(2)}) %copy-start.4) | copy-done | bytes 524312
  68.0 0.0 copy-start.5
  68.0 8.3 %weight_grads.1 = (bf16[1,3072,1024]{2,1,0:T(8,128)(2,1)}, bf16[1,3072,1024]{2,1,0:T(8,128)(2,1)}, bf16[1,1024,3072]{2,1,0:T(8,128)(2,1)}) custom-call(bf16[256,3072]{1,0:T(8,128)(2,1)S(1)} %bitcast.5, bf16[256,3072]{1,0:T(8,128)(2,1)S(1)} %bitcast.6, bf16[256,1024]{1,0:T(8,128)(2,1)S(1)} %copy-done.2, bf16[256,1024]{1,0:T(8,128)(2,1)S(1)} %copy-done.3, ...), custom_call_target="tpu_custom_call" | custom-call | flops 4831838208 | bytes 18874368 | tf_op jit(solution)/shard_map/weight_grads/pallas_call | solution.py:309
  76.2 0.0 copy-done.5
  76.2 0.6 copy.12
Async XLA Ops:
  62.0 1.4 %copy-start = (bf16[4,4,16,3072]{3,2,1,0:T(8,128)(2,1)S(1)}, bf16[4,4,16,3072]{3,2,1,0:T(8,128)(2,1)}, u32[]{:S(2)}) copy-start(bf16[4,4,16,3072]{3,2,1,0:T(8,128)(2,1)} %get-tuple-element.14) | copy-start | bytes 4718596
  63.4 1.4 %copy-start.1 = (bf16[4,4,16,3072]{3,2,1,0:T(8,128)(2,1)S(1)}, bf16[4,4,16,3072]{3,2,1,0:T(8,128)(2,1)}, u32[]{:S(2)}) copy-start(bf16[4,4,16,3072]{3,2,1,0:T(8,128)(2,1)} %get-tuple-element.15) | copy-start | bytes 4718596
  64.9 1.0 %copy-start.2 = (bf16[256,1024]{1,0:T(8,128)(2,1)S(1)}, bf16[256,1024]{1,0:T(8,128)(2,1)}, u32[]{:S(2)}) copy-start(bf16[256,1024]{1,0:T(8,128)(2,1)} %get-tuple-element.16.hid) | copy-start | bytes 1572868
  65.9 1.0 %copy-start.3 = (bf16[256,1024]{1,0:T(8,128)(2,1)S(1)}, bf16[256,1024]{1,0:T(8,128)(2,1)}, u32[]{:S(2)}) copy-start(bf16[256,1024]{1,0:T(8,128)(2,1)} %get-tuple-element.17.ggp) | copy-start | bytes 1572868
  66.9 1.0 %copy-start.4 = (bf16[256,1024]{1,0:T(8,128)(2,1)S(1)}, bf16[256,1024]{1,0:T(8,128)(2,1)}, u32[]{:S(2)}) copy-start(bf16[256,1024]{1,0:T(8,128)(2,1)} %get-tuple-element.18.gup) | copy-start | bytes 1572868
  68.0 8.3 %copy-start.5 = (bf16[16,3072]{1,0:T(8,128)(2,1)S(1)}, bf16[16,3072]{1,0:T(8,128)(2,1)}, u32[]{:S(2)}) copy-start(bf16[16,3072]{1,0:T(8,128)(2,1)} %get-tuple-element.28) | copy-start | bytes 294916

commit v2 on v1

--- a/solution.py
+++ b/solution.py
@@ -44,9 +44,9 @@
     return picks, weight
 
 
-def exchange(E, C, tok, grad, meta, wg_h, wu_h, wd_h,
+def exchange(E, C, tok, grad, ids, comb, wg_h, wu_h, wd_h,
              rin_o, rgr_o, hid_o, ggp_o, gup_o, gi_o,
-             wg, wu, wd, swap, gath, metab, sendb, X, picks, hid, ggp, gup,
+             wg, wu, wd, swap, gath, metab, sendb, X, picks, hid, ggp, gup, rin_t, hid_t,
              sibs, sibr, part, ret, tokp, zr, fin, got,
              wsem, osem, sw_s, sw_r, ga_s, ga_r, me_s, me_r, ex_s, ex_r, sx_s, sx_r,
              si_s, si_r, pa_s, pa_r, to_s, to_r, fi_s, fi_r):
@@ -66,6 +66,7 @@
             device_id={"expert": expert, "tp": tp}, device_id_type=pl.DeviceIdType.MESH)
 
     sib = z * 2 + o
+    is_in = c == 0
     weights = [pltpu.make_async_copy(a.at[0], b, wsem.at[i])
                for i, (a, b) in enumerate(((wg_h, wg), (wu_h, wu), (wd_h, wd)))]
     for w in weights:
@@ -85,10 +86,20 @@
         hello(e, q * 2 + c)
     pl.semaphore_wait(barrier, 1 + (E - 1) + (C - 1))
 
-    is_in = c == 0
     swap[...] = jnp.where(is_in, grad[...].astype(F32), tok[...].astype(F32)).astype(BF16)
     gath[z, c] = jnp.where(is_in, tok[...].astype(F32), grad[...].astype(F32)).astype(BF16)
-    metab[z, c] = meta[...]
+    metab[z, c] = jnp.zeros((8, 128), F32)
+    for i, source in enumerate((ids, comb)):
+        values = source[...].astype(F32)
+        none = jnp.zeros_like(values)
+        metab[z, c, 2 * i:2 * i + 2, :2 * n_tok] = jnp.concatenate(
+            [jnp.where(is_in, values, none), jnp.where(is_in, none, values)], axis=1)
+
+    near = jnp.minimum(z, C - 1 - z)
+
+    def position(origin):
+        far = jnp.abs(origin - z)
+        return jnp.where(far <= near, jnp.where(origin < z, 2 * far - 1, 2 * far), near + far)
     a = remote(swap, gath.at[z, c], sw_s.at[0], sw_r.at[0], e, sib)
     b = remote(metab.at[z, c], metab.at[z, c], sw_s.at[1], sw_r.at[1], e, sib)
     a.start()
@@ -109,9 +120,9 @@
     for way in (0, 1):
         pl.when(can[way])(functools.partial(send_on, z, way))
 
-    def rows_out(origin, i):
-        return remote(sendb.at[origin, peers[i]], X.at[c, origin, e],
-                      ex_s.at[origin, i], ex_r.at[origin, i], peers[i], t)
+    def rows_out(origin, i, m):
+        return remote(sendb.at[origin, peers[i]], X.at[c, m, e],
+                      ex_s.at[origin, i], ex_r.at[m, i], peers[i], t)
 
     def process(origin):
         info = metab[origin, 0] + metab[origin, 1]
@@ -122,16 +133,16 @@
         rows = dot(sel, gath[origin].reshape(2 * n_tok, D), 1, 0)
         sendb[origin] = (rows * scale).astype(BF16).reshape(E, n_tok, D)
         for i in range(E - 1):
-            rows_out(origin, i).start()
-        X[c, origin, e] = sendb[origin, e]
-
-    def sibling_rows(kind, origin):
-        return remote(X.at[kind, origin], X.at[kind, origin], sx_s.at[origin], sx_r.at[origin], e, sib)
-
-    def arrived(origin):
-        for i in range(E - 1):
-            rows_out(origin, i).wait_recv()
-        sibling_rows(c, origin).start()
+            rows_out(origin, i, position(origin)).start()
+        X[c, position(origin), e] = sendb[origin, e]
+
+    def sibling_rows(kind, m):
+        return remote(X.at[kind, m], X.at[kind, m], sx_s.at[m], sx_r.at[m], e, sib)
+
+    def arrived(m):
+        for i in range(E - 1):
+            rows_out(0, i, m).wait_recv()
+        sibling_rows(c, m).start()
 
     def take(origin, way):
         for d in hop(origin, way):
@@ -143,41 +154,42 @@
     for k in range(1, C):
         pl.when(z - k >= 0)(functools.partial(take, z - k, 0))
         pl.when(z + k < C)(functools.partial(take, z + k, 1))
-    arrived(z)
-    for k in range(1, C):
-        pl.when(z - k >= 0)(functools.partial(arrived, z - k))
-        pl.when(z + k < C)(functools.partial(arrived, z + k))
-    for q in range(C):
-        sibling_rows(o, q).wait_recv()
+    step = min(256, F)
+    part_rows = C // 2
+    half_rows = R // 2
+
+    def hidden_units(h):
+        for m in range(h * part_rows, (h + 1) * part_rows):
+            sibling_rows(o, m).wait_recv()
+        rows = pl.ds(h * half_rows, half_rows)
+
+        @pl.loop(0, F // step)
+        def _(n):
+            cols = pl.ds(pl.multiple_of(n * step, step), step)
+            rin = X[0, pl.ds(h * part_rows, part_rows)].reshape(half_rows, D)
+            rgr = X[1, pl.ds(h * part_rows, part_rows)].reshape(half_rows, D)
+            gate = dot(rin, wg[:, cols], 1, 0)
+            up = dot(rin, wu[:, cols], 1, 0)
+            gh = dot(rgr, wd[cols, :], 1, 1)
+            s = jax.nn.sigmoid(gate)
+            act = gate * s
+            hid[rows, cols] = (act * up).astype(BF16)
+            ggp[rows, cols] = (gh * up * s * (1.0 + gate * (1.0 - s))).astype(BF16)
+            gup[rows, cols] = (gh * act).astype(BF16)
+
+    for m in range(part_rows):
+        arrived(m)
     for w in weights:
         w.wait()
-
-    saves = [pltpu.make_async_copy(X.at[0], rin_o, osem.at[0]),
-             pltpu.make_async_copy(X.at[1], rgr_o, osem.at[1])]
+    hidden_units(0)
+    for m in range(part_rows, C):
+        arrived(m)
+    hidden_units(1)
+
+    saves = [pltpu.make_async_copy(a, b, osem.at[i])
+             for i, (a, b) in enumerate(((X.at[1], rgr_o), (ggp, ggp_o), (gup, gup_o)))]
     for s in saves:
         s.start()
-
-    step = min(256, F)
-
-    @pl.loop(0, F // step)
-    def _(n):
-        cols = pl.ds(pl.multiple_of(n * step, step), step)
-        rin = X[0].reshape(R, D)
-        rgr = X[1].reshape(R, D)
-        gate = dot(rin, wg[:, cols], 1, 0)
-        up = dot(rin, wu[:, cols], 1, 0)
-        gh = dot(rgr, wd[cols, :], 1, 1)
-        s = jax.nn.sigmoid(gate)
-        act = gate * s
-        hid[:, cols] = (act * up).astype(BF16)
-        ggp[:, cols] = (gh * up * s * (1.0 + gate * (1.0 - s))).astype(BF16)
-        gup[:, cols] = (gh * act).astype(BF16)
-
-    more = [pltpu.make_async_copy(a, b, osem.at[2 + i])
-            for i, (a, b) in enumerate(((hid, hid_o), (ggp, ggp_o), (gup, gup_o)))]
-    for s in more:
-        s.start()
-    saves += more
 
     def back(half, n):
         at = pl.ds(pl.multiple_of(half * W + n * cw, cw), cw)
@@ -206,8 +218,24 @@
             part_out(n, i).start()
         ret[n, e] = part[n, :, e]
 
+    @pl.loop(0, D // 256)
+    def _(n):
+        at = pl.ds(pl.multiple_of(n * 256, 256), 256)
+        rin_t[at, :] = X[0, :, :, :, at].reshape(R, 256).T
+
+    @pl.loop(0, F // 256)
+    def _(n):
+        at = pl.ds(pl.multiple_of(n * 256, 256), 256)
+        hid_t[at, :] = hid[:, at].T
+
+    turned = [pltpu.make_async_copy(a, b, osem.at[3 + i])
+              for i, (a, b) in enumerate(((rin_t, rin_o), (hid_t, hid_o)))]
+    for s in turned:
+        s.start()
+    saves += turned
+
     def to_tokens(n, q):
-        return dot(picks[q], ret[n, :, q].reshape(E * n_tok, cw), 0, 0)
+        return dot(picks[q], ret[n, :, position(q)].reshape(E * n_tok, cw), 0, 0)
 
     for n in range(PIECES):
         for i in range(E - 1):
@@ -242,7 +270,7 @@
         pl.when(jnp.logical_and(z + k < C, can[1]))(functools.partial(sent, z + k, 1))
     for q in range(C):
         for i in range(E - 1):
-            rows_out(q, i).wait_send()
+            rows_out(q, i, q).wait_send()
         sibling_rows(c, q).wait_send()
     for n in range(PIECES):
         sib_sum(n).wait_send()
@@ -257,9 +285,9 @@
 
 def weight_grads(rin, rgr, hid, ggp, gup, gg, gu, gd):
     x = rin[...]
-    gg[0] = dot(x, ggp[...], 0, 0).astype(BF16)
-    gu[0] = dot(x, gup[...], 0, 0).astype(BF16)
-    gd[0] = dot(hid[...], rgr[...], 0, 0).astype(BF16)
+    gg[0] = dot(x, ggp[...], 1, 0).astype(BF16)
+    gu[0] = dot(x, gup[...], 1, 0).astype(BF16)
+    gd[0] = dot(hid[...], rgr[...], 1, 0).astype(BF16)
 
 
 def per_device(E, T, tokens_in, grad_out, expert_ids, combine, w_gate, w_up, w_down):
@@ -268,25 +296,21 @@
     C = T // 2
     R = C * E * n_tok
     cw = D // 2 // PIECES
-    small = jnp.concatenate([expert_ids.T.astype(F32), combine.T], axis=0)
-    core = lax.axis_index("tp") % 2
-    wide = jnp.concatenate([jnp.where(core == 0, small, 0.0), jnp.where(core == 1, small, 0.0)], axis=1)
-    meta = jnp.pad(wide, ((0, 4), (0, 128 - 2 * n_tok)))
     any_, vm = pl.BlockSpec(memory_space=pl.ANY), pl.BlockSpec(memory_space=pltpu.VMEM)
     rows_t = jax.ShapeDtypeStruct((C, E, n_tok, D), BF16)
     ff_t = jax.ShapeDtypeStruct((R, F), BF16)
     V, S = pltpu.VMEM, pltpu.SemaphoreType.DMA
     rin, rgr, hid, ggp, gup, grad_input = pl.pallas_call(
         functools.partial(exchange, E, C),
-        out_shape=(rows_t, rows_t, ff_t, ff_t, ff_t, jax.ShapeDtypeStruct((n_tok, D), BF16)),
-        in_specs=[vm, vm, vm, any_, any_, any_],
+        out_shape=(jax.ShapeDtypeStruct((D, R), BF16), rows_t, jax.ShapeDtypeStruct((F, R), BF16), ff_t, ff_t, jax.ShapeDtypeStruct((n_tok, D), BF16)),
+        in_specs=[vm, vm, vm, vm, any_, any_, any_],
         out_specs=(any_, any_, any_, any_, any_, vm),
         scratch_shapes=[
             V((D, F), BF16), V((D, F), BF16), V((F, D), BF16),
             V((n_tok, D), BF16), V((C, 2, n_tok, D), BF16), V((C, 2, 8, 128), F32),
             V((C, E, n_tok, D), BF16), V((2, C, E, n_tok, D), BF16),
             V((C, E * n_tok, 2 * n_tok), BF16),
-            V((R, F), BF16), V((R, F), BF16), V((R, F), BF16),
+            V((R, F), BF16), V((R, F), BF16), V((R, F), BF16), V((D, R), BF16), V((F, R), BF16),
             V((PIECES, R, cw), BF16), V((PIECES, R, cw), BF16),
             V((PIECES, C, E, n_tok, cw), BF16), V((PIECES, E, C, n_tok, cw), BF16),
             V((PIECES, C, 2, n_tok, cw), BF16), V((PIECES, C, 2, n_tok, cw), BF16),
@@ -302,7 +326,7 @@
         cost_estimate=pl.CostEstimate(
             flops=10 * R * D * F, bytes_accessed=6 * D * F, transcendentals=R * F),
         name="exchange",
-    )(tokens_in, grad_out, meta, w_gate, w_up, w_down)
+    )(tokens_in, grad_out, expert_ids.T, combine.T, w_gate, w_up, w_down)
     block = 512
     whole = pl.BlockSpec((R, F), lambda i: (0, 0))
     cols = pl.BlockSpec((R, block), lambda i: (0, i))
@@ -311,15 +335,16 @@
         grid=(D // block,),
         out_shape=(jax.ShapeDtypeStruct((1, D, F), BF16), jax.ShapeDtypeStruct((1, D, F), BF16),
                    jax.ShapeDtypeStruct((1, F, D), BF16)),
-        in_specs=[cols, cols, whole, whole, whole],
+        in_specs=[pl.BlockSpec((block, R), lambda i: (i, 0)), cols,
+                  pl.BlockSpec((F, R), lambda i: (0, 0)), whole, whole],
         out_specs=(pl.BlockSpec((1, block, F), lambda i: (0, i, 0)),
                    pl.BlockSpec((1, block, F), lambda i: (0, i, 0)),
                    pl.BlockSpec((1, F, block), lambda i: (0, 0, i))),
-        compiler_params=pltpu.CompilerParams(vmem_limit_bytes=VMEM_BYTES // 2),
+        compiler_params=pltpu.CompilerParams(vmem_limit_bytes=VMEM_BYTES),
         cost_estimate=pl.CostEstimate(
             flops=6 * R * D * F, bytes_accessed=6 * D * F, transcendentals=0),
         name="weight_grads",
-    )(rin.reshape(R, D), rgr.reshape(R, D), hid, ggp, gup)
+    )(rin, rgr.reshape(R, D), hid, ggp, gup)
     return grad_input, gg, gu, gd
 
 

time: 77.3 us -> 70.8 us (0.916)
  local copies, waits for them, and re-layouts: 6.58 us -> 0.64 us
  other arithmetic: 2.04 us -> 0 us
  Pallas kernels: 67.6 us -> 69.2 us
    unnamed x13 -> x3, local copies, waits for them, and re-layouts: 6.58 us -> 0.64 us
    pallas_call x1, Pallas kernels: 8.26 us -> 9.82 us  [per_device(): pl.pallas_call(weight_grads, grid=(D // block,), out_shape=(jax.ShapeDtyp...]
where the time goes in v2:
time: 70.8 us; the launch traced here: 70.5 us
  Pallas kernels  69.2 us (98%)
    pallas_call x1, Pallas kernels, per_device(): pl.pallas_call(functools.partial(exchange, E, C), out_shape=(jax.ShapeDty...  59.4 us
    pallas_call x1, Pallas kernels, per_device(): pl.pallas_call(weight_grads, grid=(D // block,), out_shape=(jax.ShapeDtyp...  9.82 us

profile of v2, /device:TPU:0, one launch (start us, length us, event | category | flops | bytes accessed | tf_op | source)
XLA Modules:
  0.0 70.5 jit_solution(9961027703815203772)
XLA Ops:
  0.6 59.4 %exchange.1 = (bf16[3072,256]{1,0:T(8,128)(2,1)}, bf16[4,4,16,3072]{3,2,1,0:T(8,128)(2,1)}, bf16[1024,256]{1,0:T(8,128)(2,1)}, bf16[256,1024]{1,0:T(8,128)(2,1)}...) custom-call(bf16[16,3072]{1,0:T(8,128)(2,1)} %tok.1, bf16[16,3072]{1,0:T(8,128)(2,1)} %grad.1, s32[2,16]{1,0:T(2,128)} %bitcast.3, ...), custom_call_target="tpu_custom_call" | custom-call | flops 8053063680 | bytes 18874368 | tf_op jit(solution)/shard_map/exchange/pallas_call | solution.py:303
  60.0 0.0 copy-start
  60.0 9.8 %weight_grads.1 = (bf16[1,3072,1024]{2,1,0:T(8,128)(2,1)}, bf16[1,3072,1024]{2,1,0:T(8,128)(2,1)}, bf16[1,1024,3072]{2,1,0:T(8,128)(2,1)}) custom-call(bf16[3072,256]{1,0:T(8,128)(2,1)} %get-tuple-element.14.rin, bf16[256,3072]{1,0:T(8,128)(2,1)} %bitcast.5, bf16[1024,256]{1,0:T(8,128)(2,1)} %get-tuple-element.16.hid, ...), custom_call_target="tpu_custom_call" | custom-call | flops 4831838208 | bytes 18874368 | tf_op jit(solution)/shard_map/weight_grads/pallas_call | solution.py:333
  69.8 0.0 copy-done
  69.8 0.6 copy.12
Async XLA Ops:
  60.0 9.8 %copy-start = (bf16[16,3072]{1,0:T(8,128)(2,1)S(1)}, bf16[16,3072]{1,0:T(8,128)(2,1)}, u32[]{:S(2)}) copy-start(bf16[16,3072]{1,0:T(8,128)(2,1)} %get-tuple-element.26) | copy-start | bytes 294916

commit v3 on v2

--- a/solution.py
+++ b/solution.py
@@ -327,7 +327,7 @@
             flops=10 * R * D * F, bytes_accessed=6 * D * F, transcendentals=R * F),
         name="exchange",
     )(tokens_in, grad_out, expert_ids.T, combine.T, w_gate, w_up, w_down)
-    block = 512
+    block = 1024
     whole = pl.BlockSpec((R, F), lambda i: (0, 0))
     cols = pl.BlockSpec((R, block), lambda i: (0, i))
     gg, gu, gd = pl.pallas_call(

time: 70.8 us -> 69.8 us (0.986)
  Pallas kernels: 69.2 us -> 68.3 us
    pallas_call x1, Pallas kernels: 9.82 us -> 8.93 us  [per_device(): pl.pallas_call(weight_grads, grid=(D // block,), out_shape=(jax.ShapeDtyp...]
where the time goes in v3:
time: 69.8 us; the launch traced here: 69.6 us
  Pallas kernels  68.3 us (98%)
    pallas_call x1, Pallas kernels, per_device(): pl.pallas_call(functools.partial(exchange, E, C), out_shape=(jax.ShapeDty...  59.4 us
    pallas_call x1, Pallas kernels, per_device(): pl.pallas_call(weight_grads, grid=(D // block,), out_shape=(jax.ShapeDtyp...  8.93 us

profile of v3, /device:TPU:0, one launch (start us, length us, event | category | flops | bytes accessed | tf_op | source)
XLA Modules:
  0.0 69.6 jit_solution(6941721641441522649)
XLA Ops:
  0.6 59.4 %exchange.1 = (bf16[3072,256]{1,0:T(8,128)(2,1)}, bf16[4,4,16,3072]{3,2,1,0:T(8,128)(2,1)}, bf16[1024,256]{1,0:T(8,128)(2,1)}, bf16[256,1024]{1,0:T(8,128)(2,1)}...) custom-call(bf16[16,3072]{1,0:T(8,128)(2,1)} %tok.1, bf16[16,3072]{1,0:T(8,128)(2,1)} %grad.1, s32[2,16]{1,0:T(2,128)} %bitcast.3, ...), custom_call_target="tpu_custom_call" | custom-call | flops 8053063680 | bytes 18874368 | tf_op jit(solution)/shard_map/exchange/pallas_call | solution.py:303
  60.0 0.0 copy-start
  60.0 8.9 %weight_grads.1 = (bf16[1,3072,1024]{2,1,0:T(8,128)(2,1)}, bf16[1,3072,1024]{2,1,0:T(8,128)(2,1)}, bf16[1,1024,3072]{2,1,0:T(8,128)(2,1)}) custom-call(bf16[3072,256]{1,0:T(8,128)(2,1)} %get-tuple-element.14.rin, bf16[256,3072]{1,0:T(8,128)(2,1)} %bitcast.5, bf16[1024,256]{1,0:T(8,128)(2,1)} %get-tuple-element.16.hid, ...), custom_call_target="tpu_custom_call" | custom-call | flops 4831838208 | bytes 18874368 | tf_op jit(solution)/shard_map/weight_grads/pallas_call | solution.py:333
  68.9 0.0 copy-done
  68.9 0.6 copy.12
Async XLA Ops:
  60.0 8.9 %copy-start = (bf16[16,3072]{1,0:T(8,128)(2,1)S(1)}, bf16[16,3072]{1,0:T(8,128)(2,1)}, u32[]{:S(2)}) copy-start(bf16[16,3072]{1,0:T(8,128)(2,1)} %get-tuple-element.26) | copy-start | bytes 294916
